TPU v7x, 128 devices: a whole 4x4x4 slice. The times are simulated.
128 devices in a mesh: adapter: 32 (over x, z, core), head: 4 (over y).
Axes of the slice: x: 4, y: 4, z: 4, core: 2. Of those that a mesh axis runs over, the one named last changes fastest.
Arguments:
- call_token_inputs: bfloat16 [1024, 32, 4096], P('adapter', None, 'head'), may hold values from -6 to 6
- routed_group_index: int32 [1024], replicated, may hold values from 0 to 31, as said below
- call_adapter_index: int32 [1024, 1], replicated, may hold values from 0 to 63
- holder_table_row: int32 [64], replicated, may hold values from 0 to 63, each once
- channel_input_weight: bfloat16 [4096, 4096], P(None, 'head'), may hold values from -0.09375 to 0.09375
- input_state_weight: bfloat16 [4096, 512], P(None, 'head'), may hold values from -0.09375 to 0.09375
- output_state_weight: bfloat16 [4096, 512], P(None, 'head'), may hold values from -0.09375 to 0.09375
- step_size_weight: bfloat16 [4096, 64], P(None, 'head'), may hold values from -0.09375 to 0.09375
- channel_input_taps: bfloat16 [4, 4096], P(None, 'head'), may hold values from -3 to 3
- input_state_taps: bfloat16 [4, 512], P(None, 'head'), may hold values from -3 to 3
- output_state_taps: bfloat16 [4, 512], P(None, 'head'), may hold values from -3 to 3
- adapter_down_weight: bfloat16 [64, 4096, 64], P('adapter', None, 'head'), may hold values from -0.09375 to 0.09375
- adapter_up_weight: bfloat16 [64, 64, 4096], P('adapter', None, 'head'), may hold values from -0.75 to 0.75
- decay_logarithm: float32 [64], P('head'), may hold values from -2.5 to 1.5
- step_size_bias: float32 [64], P('head'), may hold values from -2 to 0
- head_skip_factor: float32 [64], P('head'), may hold values from 0.5 to 1.5
Outputs:
- replies: bfloat16 [2048, 32, 4096], P('adapter', None, 'head')
Inputs may be any that keep to these rules, and one draw needn't show every extreme that they name: `routed_group_index`: among the 32 calls of one source no group is named more than 2 times, and one group is named exactly 2 times by every source. `call_adapter_index`: every adapter is named by some call. `holder_table_row`: A permutation of 0 to 63.
All inputs are finite; a program needn't handle non-finite values.
Results may differ from a plain program's by a relative error of at most 0.0035.
Values may be sent and summed in bfloat16 or wider, within the bound.
A program may use at most 192 MiB of HBM per device.

v0:
```python
import jax
import jax.numpy as jnp
from jax import lax
from jax.sharding import PartitionSpec as P

HEAD_DIM = 64
NSTATE = 128
CAP = 2
PRECISE = lax.Precision.HIGHEST


def call_ranks(group_grid):
    count = group_grid.shape[-1]
    same_group = group_grid[..., :, None] == group_grid[..., None, :]
    earlier = jnp.arange(count)[None, :] < jnp.arange(count)[:, None]
    return jnp.sum(jnp.where(same_group & earlier, 1, 0), axis=-1).astype(jnp.int32)


def causal_filter_apply(series, kernel):
    span = kernel.shape[0]
    length = series.shape[1]
    padded = jnp.pad(series, ((0, 0), (span - 1, 0), (0, 0)))
    summed = jnp.zeros(series.shape, jnp.float32)
    for offset in range(span):
        summed = (
            summed + kernel[offset].astype(jnp.float32) * padded[:, offset : offset + length, :]
        )
    return jax.nn.silu(summed)


def state_space(
    filtered_inputs, b_conv, c_conv, dt_vals, decay_logarithm, head_skip_factor, call_token_length
):
    blocks = filtered_inputs.shape[0]
    block_rows = filtered_inputs.shape[1]
    head_count = decay_logarithm.shape[0]
    group_count = b_conv.shape[2] // NSTATE
    x_heads = filtered_inputs.reshape(blocks, block_rows, head_count, HEAD_DIM)
    b_groups = b_conv.reshape(blocks, block_rows, group_count, NSTATE)
    c_groups = c_conv.reshape(blocks, block_rows, group_count, NSTATE)
    step_vals = -jnp.exp(decay_logarithm) * dt_vals
    cumulated = jnp.cumsum(jnp.moveaxis(step_vals, 2, 1), axis=2)
    row_iota = jnp.arange(block_rows)
    causal = (row_iota[:, None] // call_token_length == row_iota[None, :] // call_token_length) & (
        row_iota[None, :] <= row_iota[:, None]
    )
    segment = cumulated[:, :, :, None] - cumulated[:, :, None, :]
    decay = jnp.where(causal, jnp.exp(jnp.where(causal, segment, 0.0)), 0.0)
    routing_marks = jnp.einsum("ntgk,njgk->ngtj", c_groups, b_groups, precision=PRECISE)
    routing_marks = jnp.repeat(routing_marks, head_count // group_count, axis=1)
    mixing = routing_marks * decay * jnp.moveaxis(dt_vals, 2, 1)[:, :, None, :]
    output = (
        jnp.einsum("nhtj,njhp->nthp", mixing, x_heads, precision=PRECISE)
        + head_skip_factor[:, None] * x_heads
    )
    return output.reshape(blocks, block_rows, head_count * HEAD_DIM)


def on_device(
    call_token_inputs,
    routed_group_index,
    call_adapter_index,
    holder_table_row,
    channel_input_weight,
    input_state_weight,
    output_state_weight,
    step_size_weight,
    channel_input_taps,
    input_state_taps,
    output_state_taps,
    adapter_down_weight,
    adapter_up_weight,
    decay_logarithm,
    step_size_bias,
    head_skip_factor,
):
    sender_indices = lax.axis_size("adapter")
    my_group = lax.axis_index("adapter")
    per_source = call_token_inputs.shape[0]
    call_token_length = call_token_inputs.shape[1]
    slot_count = sender_indices * CAP
    group_grid = routed_group_index.reshape(sender_indices, per_source)
    rank_grid = call_ranks(group_grid)
    call_iota = jnp.arange(per_source, dtype=jnp.int32)
    my_groups = lax.dynamic_index_in_dim(group_grid, my_group, 0, keepdims=False)
    my_ranks = lax.dynamic_index_in_dim(rank_grid, my_group, 0, keepdims=False)
    send_slot = my_groups * CAP + my_ranks
    slot_iota = jnp.arange(slot_count, dtype=jnp.int32)
    send_match = send_slot[None, :] == slot_iota[:, None]
    send_live = jnp.any(send_match, axis=1)
    send_call = jnp.sum(jnp.where(send_match, call_iota[None, :], 0), axis=1)
    rank_iota = jnp.arange(CAP, dtype=jnp.int32)
    recv_match = (group_grid[:, None, :] == my_group) & (
        rank_grid[:, None, :] == rank_iota[None, :, None]
    )
    local_call = jnp.sum(jnp.where(recv_match, call_iota[None, None, :], 0), axis=2)
    global_call = (
        jnp.arange(sender_indices, dtype=jnp.int32)[:, None] * per_source + local_call
    ).reshape(-1)
    slot_pos = holder_table_row[call_adapter_index[global_call, 0]]
    down_weight_table, up_weight_table = (
        lax.all_gather(adapter_down_weight, "adapter", axis=0, tiled=True),
        lax.all_gather(adapter_up_weight, "adapter", axis=0, tiled=True),
    )
    slot_down_weight = jnp.take(down_weight_table, slot_pos, axis=0)
    slot_up_weight = jnp.take(up_weight_table, slot_pos, axis=0)
    features = lax.all_gather(call_token_inputs, "head", axis=2, tiled=True)
    outgoing = jnp.where(
        send_live[:, None, None],
        jnp.take(features, send_call, axis=0),
        jnp.zeros((), features.dtype),
    )
    landed_rows = lax.all_to_all(outgoing, "adapter", split_axis=0, concat_axis=0, tiled=True)
    flat_rows = landed_rows.reshape(-1, landed_rows.shape[2])
    projected_inputs = jnp.dot(flat_rows, channel_input_weight, preferred_element_type=jnp.float32)
    proj_b = jnp.dot(flat_rows, input_state_weight, preferred_element_type=jnp.float32)
    proj_c = jnp.dot(flat_rows, output_state_weight, preferred_element_type=jnp.float32)
    proj_dt = jnp.dot(flat_rows, step_size_weight, preferred_element_type=jnp.float32)
    reduced_features = jnp.einsum(
        "vxg,vgj->vxj", landed_rows, slot_down_weight, preferred_element_type=jnp.float32
    )
    local_slot_count = landed_rows.shape[0]
    reduced_every_call = lax.all_gather(
        reduced_features.astype(jnp.bfloat16), "head", axis=2, tiled=True
    )
    adapter_delta_output = jnp.einsum(
        "uce,ued->ucd", reduced_every_call, slot_up_weight, preferred_element_type=jnp.float32
    )
    filtered_inputs = causal_filter_apply(
        projected_inputs.reshape(local_slot_count, call_token_length, -1) + adapter_delta_output,
        channel_input_taps,
    )
    b_conv = causal_filter_apply(
        proj_b.reshape(local_slot_count, call_token_length, -1), input_state_taps
    )
    c_conv = causal_filter_apply(
        proj_c.reshape(local_slot_count, call_token_length, -1), output_state_taps
    )
    dt_vals = jax.nn.softplus(
        proj_dt.reshape(local_slot_count, call_token_length, -1) + step_size_bias
    )
    row_total = local_slot_count * call_token_length
    block_rows = min(128, row_total)
    blocks = row_total // block_rows

    def blocked(values):
        return values.reshape(blocks, block_rows, values.shape[2])

    output = state_space(
        blocked(filtered_inputs),
        blocked(b_conv),
        blocked(c_conv),
        blocked(dt_vals),
        decay_logarithm,
        head_skip_factor,
        call_token_length,
    )
    return output.reshape(local_slot_count, call_token_length, -1).astype(jnp.bfloat16)


def solution(mesh):
    placed = (
        P("adapter", None, "head"),
        P(),
        P(),
        P(),
        P(None, "head"),
        P(None, "head"),
        P(None, "head"),
        P(None, "head"),
        P(None, "head"),
        P(None, "head"),
        P(None, "head"),
        P("adapter", None, "head"),
        P("adapter", None, "head"),
        P("head"),
        P("head"),
        P("head"),
    )
    return jax.shard_map(
        on_device, mesh=mesh, in_specs=placed, out_specs=P("adapter", None, "head"), check_vma=False
    )
```

profile of v0, /device:TPU:44, one launch (start us, length us, event | category | flops | bytes accessed | tf_op | source)
XLA Modules:
  0.0 619.2 jit_solution(13992757347904840570)
XLA Ops:
  6.5 0.0 copy-start
  6.5 0.7 all-gather.4.cloned.1.call-update
  7.3 0.0 all-gather.6.cloned.1.call-start
  7.3 0.7 all-gather.6.cloned.1.call-update
  8.0 0.0 all-gather.8.cloned.1.call-start
  8.1 0.7 all-gather.8.cloned.1.call-update
  8.8 0.8 reshape.303
  9.5 0.8 select_reduce_fusion
  10.3 0.1 select_reduce_fusion.2
  10.4 0.1 fusion.57
  10.5 83.5 %all-gather.4.cloned.1.call-done = bf16[32,32,4096]{2,1,0:T(8,128)(2,1)} async-done(((bf16[32,32,1024]{2,1,0:T(8,128)(2,1)}), bf16[32,32,4096]{2,1,0:T(8,128)(2,1)}) %all-gather.4.cloned.1.call-update) | async-done | bytes 8388624 | tf_op jit(solution)/shard_map/all_gather | solution.py:107
  94.1 10.9 %gather_fusion = bf16[64,32,4096]{2,1,0:T(8,128)(2,1)} fusion(bf16[32,32,4096]{2,1,0:T(8,128)(2,1)} %all-gather.4.cloned.1.call-done, s32[1024]{0:T(1024)S(1)} %pad_clamp_fusion.2), kind=kCustom, calls=%fused_computation | custom fusion | bytes 33554688 | tf_op jit(solution)/shard_map/jit(_take)/gather | solution.py:110
  105.0 14.4 %select_select_fusion = bf16[64,32,4096]{2,1,0:T(8,128)(2,1)} fusion(bf16[64,32,4096]{2,1,0:T(8,128)(2,1)} %gather_fusion, pred[64]{0:T(512)(128)(4,1)S(1)} %compare_and_fusion.1, pred[64]{0:T(512)(128)(4,1)S(1)} %fusion.57), kind=kLoop, calls=%fused_computation.12 | loop fusion | flops 16777216 | bytes 33554560 | tf_op jit(solution)/shard_map/jit(_where)/select_n | solution.py:108
  119.4 0.0 copy-start.11
  119.4 0.0 copy-start.4
  119.4 7.6 %all-to-all-start = ((bf16[64,32,4096]{2,1,0:T(8,128)(2,1)}), bf16[64,32,4096]{2,1,0:T(8,128)(2,1)}, u32[]{:S(2)}, u32[]{:S(2)}) async-start(bf16[64,32,4096]{2,1,0:T(8,128)(2,1)} %select_select_fusion), calls=%async_computation | async-start | bytes 33554432 | tf_op jit(solution)/shard_map/all_to_all | solution.py:113
  127.1 0.1 select_reduce_fusion.1
  127.2 0.1 copy.31
  127.3 0.1 add.182
  127.4 0.8 gather_fusion.1
  128.2 0.8 gather_fusion.2
  129.0 0.5 exponential_negate_fusion
  129.6 0.0 copy-done.10
  129.6 0.6 bitcast_convert_fusion.7
  130.2 0.6 bitcast_convert_fusion.3
  130.8 0.7 fusion.55
  131.5 0.0 copy-done.4
  131.5 0.6 slice_convert_fusion.3
  132.1 150.0 %all-gather.6.cloned.1.call-done = bf16[64,4096,16]{1,2,0:T(8,128)(2,1)} async-done(((bf16[2,4096,16]{1,2,0:T(8,128)(2,1)}), bf16[64,4096,16]{1,2,0:T(8,128)(2,1)}) %all-gather.6.cloned.1.call-update) | async-done | bytes 8388624 | tf_op jit(solution)/shard_map/all_gather | solution.py:102
  282.0 8.9 %gather_fusion.3 = bf16[64,4096,16]{1,2,0:T(8,128)(2,1)} fusion(bf16[64,4096,16]{1,2,0:T(8,128)(2,1)} %all-gather.6.cloned.1.call-done, s32[1024]{0:T(1024)S(1)} %pad_clamp_fusion), kind=kCustom, calls=%fused_computation.3 | custom fusion | bytes 16777472 | tf_op jit(solution)/shard_map/jit(_take)/gather | solution.py:105
  291.0 105.4 %all-gather.8.cloned.1.call-done = bf16[64,64,1024]{2,1,0:T(8,128)(2,1)} async-done(((bf16[2,64,1024]{2,1,0:T(8,128)(2,1)}), bf16[64,64,1024]{2,1,0:T(8,128)(2,1)}) %all-gather.8.cloned.1.call-update) | async-done | bytes 8388624 | tf_op jit(solution)/shard_map/all_gather | solution.py:103
  396.4 8.9 %gather_fusion.4 = bf16[64,64,1024]{2,1,0:T(8,128)(2,1)} fusion(bf16[64,64,1024]{2,1,0:T(8,128)(2,1)} %all-gather.8.cloned.1.call-done, s32[1024]{0:T(1024)S(1)} %pad_clamp_fusion), kind=kCustom, calls=%fused_computation.4 | custom fusion | bytes 16777472 | tf_op jit(solution)/shard_map/jit(_take)/gather | solution.py:106
  405.3 8.6 %all-to-all-done = bf16[64,32,4096]{2,1,0:T(8,128)(2,1)} async-done(((bf16[64,32,4096]{2,1,0:T(8,128)(2,1)}), bf16[64,32,4096]{2,1,0:T(8,128)(2,1)}, u32[]{:S(2)}, u32[]{:S(2)}) %all-to-all-start) | async-done | bytes 16777248 | tf_op jit(solution)/shard_map/all_to_all | solution.py:113
  413.9 10.5 %fusion.35 = bf16[64,32,16]{1,2,0:T(8,128)(2,1)S(1)} fusion(bf16[64,32,4096]{2,1,0:T(8,128)(2,1)} %all-to-all-done, bf16[64,4096,16]{1,2,0:T(8,128)(2,1)} %gather_fusion.3, pred[64]{0:T(512)(128)(4,1)S(1)} %compare_and_fusion), kind=kOutput, calls=%fused_computation.50 | convolution fusion | flops 272662528 | bytes 25231424 | tf_op jit(solution)/shard_map/vxg,vgj->vxj/dot_general | solution.py:119
  424.4 15.9 %all_gather.14 = bf16[64,32,64]{1,2,0:T(8,128)(2,1)S(1)} all-gather(bf16[64,32,16]{1,2,0:T(8,128)(2,1)S(1)} %fusion.35), channel_id=1, replica_groups=mesh['adapter'=32,'head'=4] {'head'}, dimensions={2}, use_global_device_ids=true | all-gather | bytes 327680 | tf_op jit(solution)/shard_map/all_gather | solution.py:123
  440.3 4.8 fusion.21
  445.1 24.3 %fusion.32 = f32[64,32,1024]{2,1,0:T(8,128)} fusion(f32[64,32,1024]{2,1,0:T(8,128)S(1)} %fusion.21, bf16[64,32,4096]{2,1,0:T(8,128)(2,1)} %all-to-all-done, bf16[4096,1024]{1,0:T(8,128)(2,1)} %param.20), kind=kOutput, calls=%fused_computation.41 | convolution fusion | flops 17181966336 | bytes 41943040 | tf_op jit(solution)/shard_map/dot_general | solution.py:115
  469.4 0.0 copy-done.5
  469.4 16.3 %divide_multiply_fusion = f32[64,32,1024]{2,1,0:T(8,128)} fusion(f32[64,32,1024]{2,1,0:T(8,128)} %fusion.32, f32[1024]{0:T(1024)S(1)} %bitcast.85, f32[1024]{0:T(1024)S(1)} %bitcast.86, f32[1024]{0:T(1024)S(1)} %bitcast.84, f32[1024]{0:T(1024)S(1)} %bitcast.83), kind=kLoop, calls=%fused_computation.31 | loop fusion | flops 23068672 | bytes 16793600 | tf_op jit(solution)/shard_map/jit(silu)/mul | solution.py:28
  485.7 13.3 %reshape_reshape.2 = f32[16,128,16,64]{3,2,1,0:T(8,128)} reshape(f32[64,32,1024]{2,1,0:T(8,128)} %divide_multiply_fusion) | data formatting | bytes 16777216 | tf_op jit(solution)/shard_map/reshape;reshape | solution.py:38
  499.0 13.4 %copy.35 = f32[16,128,16,64]{1,3,2,0:T(8,128)} copy(f32[16,128,16,64]{3,2,1,0:T(8,128)} %reshape_reshape.2) | data formatting | bytes 16777216 | tf_op jit(solution)/shard_map/reshape;reshape | solution.py:38
  512.4 0.0 copy-done.12
  512.4 14.7 %compare_select_fusion = f32[64,32,16]{1,2,0:T(8,128)S(1)} fusion(bf16[64,32,4096]{2,1,0:T(8,128)(2,1)} %all-to-all-done, f32[16]{0:T(128)S(1)} %copy-done.12, bf16[4096,16]{0,1:T(8,128)(2,1)S(1)} %copy-done.3), kind=kOutput, calls=%fused_computation.42 | convolution fusion | flops 268664832 | bytes 17039424 | tf_op jit(solution)/shard_map/dot_general | solution.py:118
  527.2 0.2 copy.32
  527.3 0.2 reshape.307
  527.5 0.0 copy-done.21
  527.5 0.1 multiply_bitcast_fusion
  527.8 0.0 copy-start.22
  527.8 8.3 %fusion.52 = f32[64,32,128]{2,1,0:T(8,128)S(1)} fusion(bf16[64,32,4096]{2,1,0:T(8,128)(2,1)} %all-to-all-done, bf16[4096,128]{1,0:T(8,128)(2,1)S(1)} %copy-done), kind=kOutput, calls=%fused_computation.65 | convolution fusion | flops 2147483648 | bytes 18874368 | tf_op jit(solution)/shard_map/dot_general | solution.py:117
  536.1 0.6 divide_multiply_fusion.2
  536.7 0.0 copy-done.22
  536.7 0.0 copy-start.13
  536.7 0.0 copy-start.14
  536.7 0.0 copy-start.15
  536.8 0.0 copy-start.16
  536.8 0.0 copy-start.9
  536.8 0.0 copy-start.24
  536.8 8.2 %fusion.50 = f32[64,32,128]{2,1,0:T(8,128)S(1)} fusion(bf16[64,32,4096]{2,1,0:T(8,128)(2,1)} %all-to-all-done, bf16[4096,128]{1,0:T(8,128)(2,1)S(1)} %copy-done.22), kind=kOutput, calls=%fused_computation.63 | convolution fusion | flops 2147483648 | bytes 18874368 | tf_op jit(solution)/shard_map/dot_general | solution.py:116
  545.0 0.6 divide_multiply_fusion.1
  545.6 2.3 fusion.67
  547.9 4.5 reduce_window_sum.11
  552.5 38.2 %fusion.13 = bf16[16,128,16,64]{1,3,2,0:T(8,128)(2,1)} fusion(f32[16,128,16,64]{1,3,2,0:T(8,128)} %copy.35, f32[16]{0:T(128)S(1)} %copy-done.24, f32[16,16,128]{2,1,0:T(8,128)S(1)} %copy.34, f32[16,16,128]{2,1,0:T(8,128)S(1)} %reduce_window_sum.11, f32[16,128,128]{2,1,0:T(8,128)S(1)} %fusion.67, pred[128,128]{1,0:T(8,128)(4,1)S(1)} %copy-done.9), kind=kOutput, calls=%fused_computation.23 | convolution fusion | flops 3248488448 | bytes 13910080 | tf_op jit(solution)/shard_map/nhtj,njhp->nthp/dot_general | solution.py:53
  590.7 10.1 %copy.37 = bf16[16,128,16,64]{3,2,1,0:T(8,128)(2,1)} copy(bf16[16,128,16,64]{1,3,2,0:T(8,128)(2,1)} %fusion.13) | data formatting | bytes 8388608 | tf_op jit(solution)/shard_map/convert_element_type | solution.py:158
  600.8 11.9 %convert_element_type.160 = bf16[64,32,1024]{2,1,0:T(8,128)(2,1)} reshape(bf16[16,128,16,64]{3,2,1,0:T(8,128)(2,1)} %copy.37) | data formatting | bytes 8388608 | tf_op jit(solution)/shard_map/convert_element_type | solution.py:158
  (52 shorter events, 0.3 us)
Async XLA Ops:
  6.5 521.2 %copy-start = (bf16[4096,128]{1,0:T(8,128)(2,1)S(1)}, bf16[4096,128]{1,0:T(8,128)(2,1)}, u32[]{:S(2)}) copy-start(bf16[4096,128]{1,0:T(8,128)(2,1)} %param.22) | copy-start | bytes 3145732
  6.5 87.5 %all-gather.4.cloned.1.call-start = ((), (), s32[]{:S(2)}) async-start(), calls=%async_computation.1 | async-start | bytes 10485760 | tf_op jit(solution)/shard_map/all_gather | solution.py:107
  7.3 274.8 %all-gather.6.cloned.1.call-start = ((), (), s32[]{:S(2)}) async-start(), calls=%async_computation.2 | async-start | bytes 8650752 | tf_op jit(solution)/shard_map/all_gather | solution.py:102
  8.0 388.4 %all-gather.8.cloned.1.call-start = ((), (), s32[]{:S(2)}) async-start(), calls=%async_computation.3 | async-start | bytes 8650752 | tf_op jit(solution)/shard_map/all_gather | solution.py:103
  119.4 8.0 %copy-start.2 = (s32[1024,1]{0,1:T(1,128)S(1)}, s32[1024,1]{0,1:T(1,128)}, u32[]{:S(2)}) copy-start(s32[1024,1]{0,1:T(1,128)} %param.18) | copy-start | bytes 12292
  119.4 8.8 %copy-start.1 = (s32[64]{0:T(128)S(1)}, s32[64]{0:T(128)}, u32[]{:S(2)}) copy-start(s32[64]{0:T(128)} %param.19) | copy-start | bytes 772
  119.4 9.7 %copy-start.23 = (f32[16]{0:T(128)S(1)}, f32[16]{0:T(128)}, u32[]{:S(2)}) copy-start(f32[16]{0:T(128)} %param.29) | copy-start | bytes 196
  119.4 10.2 %copy-start.10 = (bf16[4,128]{1,0:T(4,128)(2,1)S(1)}, bf16[4,128]{1,0:T(4,128)(2,1)}, u32[]{:S(2)}) copy-start(bf16[4,128]{1,0:T(4,128)(2,1)} %param.26) | copy-start | bytes 3076
  119.4 10.8 %copy-start.11 = (bf16[4,128]{1,0:T(4,128)(2,1)S(1)}, bf16[4,128]{1,0:T(4,128)(2,1)}, u32[]{:S(2)}) copy-start(bf16[4,128]{1,0:T(4,128)(2,1)} %param.25) | copy-start | bytes 3076
  119.4 12.1 %copy-start.4 = (bf16[4,1024]{1,0:T(4,128)(2,1)S(1)}, bf16[4,1024]{1,0:T(4,128)(2,1)}, u32[]{:S(2)}) copy-start(bf16[4,1024]{1,0:T(4,128)(2,1)} %param.24) | copy-start | bytes 24580
  119.4 294.5 %all-to-all-start = ((bf16[64,32,4096]{2,1,0:T(8,128)(2,1)}), bf16[64,32,4096]{2,1,0:T(8,128)(2,1)}, u32[]{:S(2)}, u32[]{:S(2)}) async-start(bf16[64,32,4096]{2,1,0:T(8,128)(2,1)} %select_select_fusion), calls=%async_computation | async-start | bytes 33554432 | tf_op jit(solution)/shard_map/all_to_all | solution.py:113
  445.1 24.3 %copy-start.5 = (f32[1,1024]{1,0:T(1,128)S(1)}, f32[1,1024]{1,0:T(1,128)}, u32[]{:S(2)}) copy-start(f32[1,1024]{1,0:T(1,128)} %get-tuple-element.5) | copy-start | bytes 12292
  445.1 24.3 %copy-start.6 = (f32[1,1024]{1,0:T(1,128)S(1)}, f32[1,1024]{1,0:T(1,128)}, u32[]{:S(2)}) copy-start(f32[1,1024]{1,0:T(1,128)} %get-tuple-element.6) | copy-start | bytes 12292
  445.1 24.3 %copy-start.7 = (f32[1,1024]{1,0:T(1,128)S(1)}, f32[1,1024]{1,0:T(1,128)}, u32[]{:S(2)}) copy-start(f32[1,1024]{1,0:T(1,128)} %get-tuple-element.7) | copy-start | bytes 12292
  445.1 24.3 %copy-start.8 = (f32[1,1024]{1,0:T(1,128)S(1)}, f32[1,1024]{1,0:T(1,128)}, u32[]{:S(2)}) copy-start(f32[1,1024]{1,0:T(1,128)} %get-tuple-element.8) | copy-start | bytes 12292
  499.0 13.4 %copy-start.3 = (bf16[4096,16]{0,1:T(8,128)(2,1)S(1)}, bf16[4096,16]{0,1:T(8,128)(2,1)}, u32[]{:S(2)}) copy-start(bf16[4096,16]{0,1:T(8,128)(2,1)} %param.23) | copy-start | bytes 393220
  499.0 13.4 %copy-start.12 = (f32[16]{0:T(128)S(1)}, f32[16]{0:T(128)}, u32[]{:S(2)}) copy-start(f32[16]{0:T(128)} %param.30) | copy-start | bytes 196
  512.4 15.1 %copy-start.21 = (f32[16]{0:T(128)S(1)}, f32[16]{0:T(128)}, u32[]{:S(2)}) copy-start(f32[16]{0:T(128)} %exponential_negate_fusion) | copy-start | bytes 196
  527.7 8.3 %copy-start.17 = (f32[128]{0:T(128)S(1)}, f32[128]{0:T(128)}, u32[]{:S(2)}) copy-start(f32[128]{0:T(128)} %get-tuple-element.13) | copy-start | bytes 1540
  527.7 8.3 %copy-start.18 = (f32[128]{0:T(128)S(1)}, f32[128]{0:T(128)}, u32[]{:S(2)}) copy-start(f32[128]{0:T(128)} %get-tuple-element.14) | copy-start | bytes 1540
  527.7 8.3 %copy-start.19 = (f32[128]{0:T(128)S(1)}, f32[128]{0:T(128)}, u32[]{:S(2)}) copy-start(f32[128]{0:T(128)} %get-tuple-element.15) | copy-start | bytes 1540
  527.8 8.3 %copy-start.20 = (f32[128]{0:T(128)S(1)}, f32[128]{0:T(128)}, u32[]{:S(2)}) copy-start(f32[128]{0:T(128)} %get-tuple-element.16) | copy-start | bytes 1540
  527.8 8.9 %copy-start.22 = (bf16[4096,128]{1,0:T(8,128)(2,1)S(1)}, bf16[4096,128]{1,0:T(8,128)(2,1)}, u32[]{:S(2)}) copy-start(bf16[4096,128]{1,0:T(8,128)(2,1)} %param.21) | copy-start | bytes 3145732
  536.7 8.3 %copy-start.13 = (f32[128]{0:T(128)S(1)}, f32[128]{0:T(128)}, u32[]{:S(2)}) copy-start(f32[128]{0:T(128)} %get-tuple-element.9) | copy-start | bytes 1540
  536.7 8.3 %copy-start.14 = (f32[128]{0:T(128)S(1)}, f32[128]{0:T(128)}, u32[]{:S(2)}) copy-start(f32[128]{0:T(128)} %get-tuple-element.10) | copy-start | bytes 1540
  536.7 8.3 %copy-start.15 = (f32[128]{0:T(128)S(1)}, f32[128]{0:T(128)}, u32[]{:S(2)}) copy-start(f32[128]{0:T(128)} %get-tuple-element.11) | copy-start | bytes 1540
  536.8 8.3 %copy-start.16 = (f32[128]{0:T(128)S(1)}, f32[128]{0:T(128)}, u32[]{:S(2)}) copy-start(f32[128]{0:T(128)} %get-tuple-element.12) | copy-start | bytes 1540
  536.8 15.7 %copy-start.9 = (pred[128,128]{1,0:T(8,128)(4,1)S(1)}, pred[128,128]{1,0:T(8,128)(4,1)}, u32[]{:S(2)}) copy-start(pred[128,128]{1,0:T(8,128)(4,1)} %fusion.55) | copy-start | bytes 49156
  536.8 15.7 %copy-start.24 = (f32[16]{0:T(128)S(1)}, f32[16]{0:T(128)}, u32[]{:S(2)}) copy-start(f32[16]{0:T(128)} %param.31) | copy-start | bytes 196
Sparse Core Ops, SparseCore 0:
  9.0 84.9 all-gather.3
  96.3 185.6 all-gather.5
  284.3 112.0 all-gather.7
where the time goes:
time: 621 us; the launch traced here: 619 us
  waiting for transfers between devices  350 us (56%)
  matrix products  111 us (18%)
  local copies, waits for them, and re-layouts  80.4 us (13%)
  other arithmetic  40.8 us (7%)
  blocking collectives  15.9 us (3%)
  between operations  13.6 us (2%)
  starting transfers between devices  7.7 us (1%)
    all_gather x1, waiting for transfers between devices, on_device(): lax.all_gather(adapter_down_weight, 'adapter', axis=0, tiled=True)  150 us
    all_gather x1, waiting for transfers between devices, on_device(): lax.all_gather(adapter_up_weight, 'adapter', axis=0, tiled=True)  105 us
    all_gather x1, waiting for transfers between devices, on_device(): features = lax.all_gather(call_token_inputs, 'head', axis=2, tiled=True)  83.5 us
    dot_general x1, matrix products, state_space(): jnp.einsum('nhtj,njhp->nthp', mixing, x_heads, precision=PRECISE)  38.2 us
    another operation x2, local copies, waits for them, and re-layouts, state_space(): x_heads = filtered_inputs.reshape(blocks, block_rows, head_count, HEAD_DIM)  26.7 us
    dot_general x1, matrix products, on_device(): jnp.dot(flat_rows, channel_input_weight, preferred_element_type=jnp.float32)  24.3 us
    convert_element_type x2, local copies, waits for them, and re-layouts, on_device(): output.reshape(local_slot_count, call_token_length, -1).astype(jnp.bfloat16)  21.9 us
    mul x3, other arithmetic, causal_filter_apply(): return jax.nn.silu(summed)  17.5 us
  transfers between devices with their start and end apart: 4, of which 4 were waited for; matrix products, arithmetic and copies ran while one was open for 8% of the time, Pallas kernels for 0%

commit v1 on v0

--- a/solution.py
+++ b/solution.py
@@ -104,7 +104,12 @@
     )
     slot_down_weight = jnp.take(down_weight_table, slot_pos, axis=0)
     slot_up_weight = jnp.take(up_weight_table, slot_pos, axis=0)
-    features = lax.all_gather(call_token_inputs, "head", axis=2, tiled=True)
+    ring = [call_token_inputs]
+    for hop in range(3):
+        ring.append(lax.ppermute(ring[-1], "head", [(dev, (dev + 1) % 4) for dev in range(4)]))
+    features = jnp.roll(
+        jnp.concatenate(ring[::-1], axis=2), (lax.axis_index("head") + 1) * ring[0].shape[2], axis=2
+    )
     outgoing = jnp.where(
         send_live[:, None, None],
         jnp.take(features, send_call, axis=0),

time: 621 us -> 696 us (1.12); the launches traced: 619 us -> 683 us
  waiting for transfers between devices: 350 us -> 382 us
  local copies, waits for them, and re-layouts: 80.4 us -> 109 us
    all_to_all x1, waiting for transfers between devices: 8.6 us -> 247 us  [on_device(): lax.all_to_all(outgoing, 'adapter', split_axis=0, concat_axis=0, tiled=True)]
    all_gather x1, waiting for transfers between devices: 150 us -> 0.01 us  [on_device(): lax.all_gather(adapter_down_weight, 'adapter', axis=0, tiled=True)]
    ppermute x0 -> x3, waiting for transfers between devices: none -> 135 us  [on_device(): lax.ppermute(ring[-1], 'head', [(dev, (dev + 1) % 4) for dev in range(4)])]
    all_gather x1, waiting for transfers between devices: 105 us -> 0.01 us  [on_device(): lax.all_gather(adapter_up_weight, 'adapter', axis=0, tiled=True)]
    all_gather x1 -> x0, waiting for transfers between devices: 83.5 us -> none  [on_device(): features = lax.all_gather(call_token_inputs, 'head', axis=2, tiled=True)]
    unnamed x50 -> x67, local copies, waits for them, and re-layouts: 0.11 us -> 18.9 us
    dynamic_slice x0 -> x1, local copies, waits for them, and re-layouts: none -> 7.74 us  [on_device(): jnp.roll(jnp.concatenate(ring[::-1], axis=2), (lax.axis_index('head') + 1...]
  transfers between devices with their start and end apart: 4 -> 6, of which waited for: 4 -> 4; matrix products, arithmetic and copies ran while one was open for 8% -> 11% of each run, Pallas kernels for 0% -> 0%
where the time goes in v1:
time: 696 us; the launch traced here: 683 us
  waiting for transfers between devices  382 us (55%)
  local copies, waits for them, and re-layouts  109 us (16%)
  matrix products  108 us (16%)
  other arithmetic  41 us (6%)
  blocking collectives  14.8 us (2%)
  between operations  14.3 us (2%)
  starting transfers between devices  13.2 us (2%)
    all_to_all x1, waiting for transfers between devices, on_device(): lax.all_to_all(outgoing, 'adapter', split_axis=0, concat_axis=0, tiled=True)  247 us
    ppermute x3, waiting for transfers between devices, on_device(): lax.ppermute(ring[-1], 'head', [(dev, (dev + 1) % 4) for dev in range(4)])  135 us
    dot_general x1, matrix products, state_space(): jnp.einsum('nhtj,njhp->nthp', mixing, x_heads, precision=PRECISE)  35.1 us
    another operation x2, local copies, waits for them, and re-layouts, state_space(): x_heads = filtered_inputs.reshape(blocks, block_rows, head_count, HEAD_DIM)  26.7 us
    dot_general x1, matrix products, on_device(): jnp.dot(flat_rows, channel_input_weight, preferred_element_type=jnp.float32)  24.3 us
    convert_element_type x2, local copies, waits for them, and re-layouts, on_device(): output.reshape(local_slot_count, call_token_length, -1).astype(jnp.bfloat16)  22 us
    unnamed x67, local copies, waits for them, and re-layouts  18.9 us
    mul x3, other arithmetic, causal_filter_apply(): return jax.nn.silu(summed)  17.6 us
  transfers between devices with their start and end apart: 6, of which 4 were waited for; matrix products, arithmetic and copies ran while one was open for 11% of the time, Pallas kernels for 0%

profile of v1, /device:TPU:44, one launch (start us, length us, event | category | flops | bytes accessed | tf_op | source)
XLA Modules:
  0.0 682.6 jit_solution(10476989206198097374)
XLA Ops:
  6.5 0.7 all-gather.3.cloned.1.call-update
  7.3 0.0 all-gather.5.cloned.1.call-start
  7.3 1.6 collective-permute-start
  9.0 46.0 %collective-permute-done = bf16[32,32,1024]{2,1,0:T(8,128)(2,1)S(1)} collective-permute-done((bf16[32,32,1024]{2,1,0:T(8,128)(2,1)}, bf16[32,32,1024]{2,1,0:T(8,128)(2,1)S(1)}, u32[]{:S(2)}, u32[]{:S(2)}) %collective-permute-start) | collective-permute-done | bytes 2097184 | tf_op jit(solution)/shard_map/ppermute | solution.py:109
  55.0 1.3 copy-done.4
  56.3 1.6 collective-permute-start.1
  57.9 45.1 %collective-permute-done.1 = bf16[32,32,1024]{2,1,0:T(8,128)(2,1)} collective-permute-done((bf16[32,32,1024]{2,1,0:T(8,128)(2,1)S(1)}, bf16[32,32,1024]{2,1,0:T(8,128)(2,1)}, u32[]{:S(2)}, u32[]{:S(2)}) %collective-permute-start.1) | collective-permute-done | bytes 2097184 | tf_op jit(solution)/shard_map/ppermute | solution.py:109
  103.0 1.6 collective-permute-start.2
  104.6 0.0 all-gather.5.cloned.1.call-update
  104.6 0.8 reshape.303
  105.4 0.8 select_reduce_fusion
  106.2 0.1 select_reduce_fusion.2
  106.3 0.1 fusion.57
  106.4 43.7 %collective-permute-done.2 = bf16[32,32,1024]{2,1,0:T(8,128)(2,1)} collective-permute-done((bf16[32,32,1024]{2,1,0:T(8,128)(2,1)}, bf16[32,32,1024]{2,1,0:T(8,128)(2,1)}, u32[]{:S(2)}, u32[]{:S(2)}) %collective-permute-start.2) | collective-permute-done | bytes 2097184 | tf_op jit(solution)/shard_map/ppermute | solution.py:109
  150.1 3.3 constant_dynamic-update-slice_fusion.7
  153.4 3.3 constant_dynamic-update-slice_fusion.6
  156.7 1.5 constant_dynamic-update-slice_fusion.5
  158.2 1.5 constant_dynamic-update-slice_fusion.4
  159.7 3.2 constant_dynamic-update-slice_fusion.3
  162.9 3.2 constant_dynamic-update-slice_fusion.2
  166.1 1.5 constant_dynamic-update-slice_fusion.1
  167.6 1.6 constant_dynamic-update-slice_fusion
  169.2 7.7 %constant_dynamic-slice_fusion = bf16[32,32,4096]{2,1,0:T(8,128)(2,1)} fusion(bf16[32,32,8192]{2,1,0:T(8,128)(2,1)} %constant_dynamic-update-slice_fusion, s32[]{:T(128)S(6)} %select_n.135), kind=kLoop, calls=%fused_computation.109 | loop fusion | bytes 16777220 | tf_op jit(solution)/shard_map/jit(_roll_dynamic)/dynamic_slice | solution.py:110
  176.9 10.9 %gather_fusion = bf16[64,32,4096]{2,1,0:T(8,128)(2,1)} fusion(bf16[32,32,4096]{2,1,0:T(8,128)(2,1)} %constant_dynamic-slice_fusion, s32[1024]{0:T(1024)S(1)} %pad_clamp_fusion.2), kind=kCustom, calls=%fused_computation | custom fusion | bytes 33554688 | tf_op jit(solution)/shard_map/jit(_take)/gather | solution.py:115
  187.8 14.3 %select_select_fusion = bf16[64,32,4096]{2,1,0:T(8,128)(2,1)} fusion(bf16[64,32,4096]{2,1,0:T(8,128)(2,1)} %gather_fusion, pred[64]{0:T(512)(128)(4,1)S(1)} %compare_and_fusion.1, pred[64]{0:T(512)(128)(4,1)S(1)} %fusion.57), kind=kLoop, calls=%fused_computation.12 | loop fusion | flops 16777216 | bytes 33554560 | tf_op jit(solution)/shard_map/jit(_where)/select_n | solution.py:113
  202.2 0.0 copy-start.14
  202.2 0.0 copy-start.7
  202.2 8.4 %all-to-all-start = ((bf16[64,32,4096]{2,1,0:T(8,128)(2,1)}), bf16[64,32,4096]{2,1,0:T(8,128)(2,1)}, u32[]{:S(2)}, u32[]{:S(2)}) async-start(bf16[64,32,4096]{2,1,0:T(8,128)(2,1)} %select_select_fusion), calls=%async_computation | async-start | bytes 33554432 | tf_op jit(solution)/shard_map/all_to_all | solution.py:118
  210.6 0.1 select_reduce_fusion.1
  210.7 0.1 copy.31
  210.8 0.1 add.198
  210.9 0.8 gather_fusion.1
  211.7 0.8 gather_fusion.2
  212.6 0.6 exponential_negate_fusion
  213.2 0.6 bitcast_convert_fusion.7
  213.7 0.6 bitcast_convert_fusion.3
  214.3 0.7 fusion.55
  215.0 0.6 slice_convert_fusion.3
  215.7 8.9 %gather_fusion.3 = bf16[64,4096,16]{1,2,0:T(8,128)(2,1)} fusion(bf16[64,4096,16]{1,2,0:T(8,128)(2,1)} %all-gather.3.cloned.1.call-done, s32[1024]{0:T(1024)S(1)} %pad_clamp_fusion), kind=kCustom, calls=%fused_computation.3 | custom fusion | bytes 16777472 | tf_op jit(solution)/shard_map/jit(_take)/gather | solution.py:105
  224.6 8.9 %gather_fusion.4 = bf16[64,64,1024]{2,1,0:T(8,128)(2,1)} fusion(bf16[64,64,1024]{2,1,0:T(8,128)(2,1)} %all-gather.5.cloned.1.call-done, s32[1024]{0:T(1024)S(1)} %pad_clamp_fusion), kind=kCustom, calls=%fused_computation.4 | custom fusion | bytes 16777472 | tf_op jit(solution)/shard_map/jit(_take)/gather | solution.py:106
  233.5 246.8 %all-to-all-done = bf16[64,32,4096]{2,1,0:T(8,128)(2,1)} async-done(((bf16[64,32,4096]{2,1,0:T(8,128)(2,1)}), bf16[64,32,4096]{2,1,0:T(8,128)(2,1)}, u32[]{:S(2)}, u32[]{:S(2)}) %all-to-all-start) | async-done | bytes 16777248 | tf_op jit(solution)/shard_map/all_to_all | solution.py:118
  480.3 10.6 %fusion.35 = bf16[64,32,16]{1,2,0:T(8,128)(2,1)S(1)} fusion(bf16[64,32,4096]{2,1,0:T(8,128)(2,1)} %all-to-all-done, bf16[64,4096,16]{1,2,0:T(8,128)(2,1)} %gather_fusion.3, pred[64]{0:T(512)(128)(4,1)S(1)} %compare_and_fusion), kind=kOutput, calls=%fused_computation.50 | convolution fusion | flops 272662528 | bytes 25231424 | tf_op jit(solution)/shard_map/vxg,vgj->vxj/dot_general | solution.py:124
  490.9 14.8 %all_gather.10 = bf16[64,32,64]{1,2,0:T(8,128)(2,1)S(1)} all-gather(bf16[64,32,16]{1,2,0:T(8,128)(2,1)S(1)} %fusion.35), channel_id=1, replica_groups=mesh['adapter'=32,'head'=4] {'head'}, dimensions={2}, use_global_device_ids=true | all-gather | bytes 327680 | tf_op jit(solution)/shard_map/all_gather | solution.py:128
  505.7 4.8 fusion.21
  510.5 24.3 %fusion.32 = f32[64,32,1024]{2,1,0:T(8,128)} fusion(f32[64,32,1024]{2,1,0:T(8,128)S(1)} %fusion.21, bf16[64,32,4096]{2,1,0:T(8,128)(2,1)} %all-to-all-done, bf16[4096,1024]{1,0:T(8,128)(2,1)} %param.20), kind=kOutput, calls=%fused_computation.41 | convolution fusion | flops 17181966336 | bytes 41943040 | tf_op jit(solution)/shard_map/dot_general | solution.py:120
  534.8 16.3 %divide_multiply_fusion = f32[64,32,1024]{2,1,0:T(8,128)} fusion(f32[64,32,1024]{2,1,0:T(8,128)} %fusion.32, f32[1024]{0:T(1024)S(1)} %bitcast.87, f32[1024]{0:T(1024)S(1)} %bitcast.88, f32[1024]{0:T(1024)S(1)} %bitcast.86, f32[1024]{0:T(1024)S(1)} %bitcast.85), kind=kLoop, calls=%fused_computation.31 | loop fusion | flops 23068672 | bytes 16793600 | tf_op jit(solution)/shard_map/jit(silu)/mul | solution.py:28
  551.1 13.3 %reshape_reshape.2 = f32[16,128,16,64]{3,2,1,0:T(8,128)} reshape(f32[64,32,1024]{2,1,0:T(8,128)} %divide_multiply_fusion) | data formatting | bytes 16777216 | tf_op jit(solution)/shard_map/reshape;reshape | solution.py:38
  564.4 13.4 %copy.35 = f32[16,128,16,64]{1,3,2,0:T(8,128)} copy(f32[16,128,16,64]{3,2,1,0:T(8,128)} %reshape_reshape.2) | data formatting | bytes 16777216 | tf_op jit(solution)/shard_map/reshape;reshape | solution.py:38
  577.8 14.5 %compare_select_fusion = f32[64,32,16]{1,2,0:T(8,128)S(1)} fusion(bf16[64,32,4096]{2,1,0:T(8,128)(2,1)} %all-to-all-done, f32[16]{0:T(128)S(1)} %copy-done.15, bf16[4096,16]{0,1:T(8,128)(2,1)S(1)} %copy-done.6), kind=kOutput, calls=%fused_computation.42 | convolution fusion | flops 268664832 | bytes 17039424 | tf_op jit(solution)/shard_map/dot_general | solution.py:123
  592.3 0.2 copy.32
  592.5 0.2 reshape.307
  592.7 0.1 multiply_bitcast_fusion
  592.9 4.8 reduce_window_sum.11
  597.7 0.0 copy-start.25
  597.7 8.3 %fusion.52 = f32[64,32,128]{2,1,0:T(8,128)S(1)} fusion(bf16[64,32,4096]{2,1,0:T(8,128)(2,1)} %all-to-all-done, bf16[4096,128]{1,0:T(8,128)(2,1)S(1)} %copy-done), kind=kOutput, calls=%fused_computation.65 | convolution fusion | flops 2147483648 | bytes 18874368 | tf_op jit(solution)/shard_map/dot_general | solution.py:122
  606.0 0.6 divide_multiply_fusion.2
  606.7 0.0 copy-start.12
  606.7 0.0 copy-start.27
  606.7 8.5 %fusion.50 = f32[64,32,128]{2,1,0:T(8,128)S(1)} fusion(bf16[64,32,4096]{2,1,0:T(8,128)(2,1)} %all-to-all-done, bf16[4096,128]{1,0:T(8,128)(2,1)S(1)} %copy-done.25), kind=kOutput, calls=%fused_computation.63 | convolution fusion | flops 2147483648 | bytes 18874368 | tf_op jit(solution)/shard_map/dot_general | solution.py:121
  615.3 0.6 divide_multiply_fusion.1
  616.0 2.3 fusion.70
  618.3 35.1 %fusion.13 = bf16[16,128,16,64]{1,3,2,0:T(8,128)(2,1)} fusion(f32[16,128,16,64]{1,3,2,0:T(8,128)S(1)} %bitcast.81, f32[16]{0:T(128)S(1)} %copy-done.27, f32[16,16,128]{2,1,0:T(8,128)S(1)} %copy.34, f32[16,16,128]{2,1,0:T(8,128)S(1)} %reduce_window_sum.11, f32[16,128,128]{2,1,0:T(8,128)S(1)} %fusion.70, pred[128,128]{1,0:T(8,128)(4,1)S(1)} %copy-done.12), kind=kOutput, calls=%fused_computation.23 | convolution fusion | flops 3248488448 | bytes 13910080 | tf_op jit(solution)/shard_map/nhtj,njhp->nthp/dot_general | solution.py:53
  653.4 10.1 %copy.37 = bf16[16,128,16,64]{3,2,1,0:T(8,128)(2,1)} copy(bf16[16,128,16,64]{1,3,2,0:T(8,128)(2,1)} %fusion.13) | data formatting | bytes 8388608 | tf_op jit(solution)/shard_map/convert_element_type | solution.py:163
  663.5 11.9 %convert_element_type.160 = bf16[64,32,1024]{2,1,0:T(8,128)(2,1)} reshape(bf16[16,128,16,64]{3,2,1,0:T(8,128)(2,1)} %copy.37) | data formatting | bytes 8388608 | tf_op jit(solution)/shard_map/convert_element_type | solution.py:163
  (75 shorter events, 0.3 us)
Async XLA Ops:
  6.5 591.1 %copy-start = (bf16[4096,128]{1,0:T(8,128)(2,1)S(1)}, bf16[4096,128]{1,0:T(8,128)(2,1)}, u32[]{:S(2)}) copy-start(bf16[4096,128]{1,0:T(8,128)(2,1)} %param.22) | copy-start | bytes 3145732
  6.5 151.7 %copy-start.3 = (bf16[32,32,1024]{2,1,0:T(8,128)(2,1)S(1)}, bf16[32,32,1024]{2,1,0:T(8,128)(2,1)}, u32[]{:S(2)}) copy-start(bf16[32,32,1024]{2,1,0:T(8,128)(2,1)} %param.16) | copy-start | bytes 6291460
  6.5 209.1 %all-gather.3.cloned.1.call-start = ((), (), s32[]{:S(2)}) async-start(), calls=%async_computation.1 | async-start | bytes 8650752 | tf_op jit(solution)/shard_map/all_gather | solution.py:102
  7.3 217.3 %all-gather.5.cloned.1.call-start = ((), (), s32[]{:S(2)}) async-start(), calls=%async_computation.2 | async-start | bytes 8650752 | tf_op jit(solution)/shard_map/all_gather | solution.py:103
  7.3 47.6 %collective-permute-start = (bf16[32,32,1024]{2,1,0:T(8,128)(2,1)}, bf16[32,32,1024]{2,1,0:T(8,128)(2,1)S(1)}, u32[]{:S(2)}, u32[]{:S(2)}) collective-permute-start(bf16[32,32,1024]{2,1,0:T(8,128)(2,1)} %param.16), channel_id=1, source_target_pairs={{0,1},{1,2},{2,3},{3,0},{4,5},{5,6},{6,7},{7,4},{8,9},{9,10},{10,1... | collective-permute-start | bytes 6291464 | tf_op jit(solution)/shard_map/ppermute | solution.py:109
  55.0 1.3 copy-start.4
  56.3 46.7 %collective-permute-start.1 = (bf16[32,32,1024]{2,1,0:T(8,128)(2,1)S(1)}, bf16[32,32,1024]{2,1,0:T(8,128)(2,1)}, u32[]{:S(2)}, u32[]{:S(2)}) collective-permute-start(bf16[32,32,1024]{2,1,0:T(8,128)(2,1)S(1)} %collective-permute-done), channel_id=1, source_target_pairs={{0,1},{1,2},{2,3},{3,0},{4,5},{5,6},{6,7},{7,4},{8,9},{9,10},{10,1... | collective-permute-start | bytes 6291464 | tf_op jit(solution)/shard_map/ppermute | solution.py:109
  103.0 47.1 %collective-permute-start.2 = (bf16[32,32,1024]{2,1,0:T(8,128)(2,1)}, bf16[32,32,1024]{2,1,0:T(8,128)(2,1)}, u32[]{:S(2)}, u32[]{:S(2)}) collective-permute-start(bf16[32,32,1024]{2,1,0:T(8,128)(2,1)} %collective-permute-done.1), channel_id=1, source_target_pairs={{0,1},{1,2},{2,3},{3,0},{4,5},{5,6},{6,7},{7,4},{8,9},{9,10},{10,1... | collective-permute-start | bytes 6291464 | tf_op jit(solution)/shard_map/ppermute | solution.py:109
  105.4 51.4 %copy-start.5 = (bf16[32,32,1024]{2,1,0:T(8,128)(2,1)S(1)}, bf16[32,32,1024]{2,1,0:T(8,128)(2,1)}, u32[]{:S(2)}) copy-start(bf16[32,32,1024]{2,1,0:T(8,128)(2,1)} %copy-done.4) | copy-start | bytes 6291460
  202.2 8.8 %copy-start.2 = (s32[1024,1]{0,1:T(1,128)S(1)}, s32[1024,1]{0,1:T(1,128)}, u32[]{:S(2)}) copy-start(s32[1024,1]{0,1:T(1,128)} %param.18) | copy-start | bytes 12292
  202.2 9.6 %copy-start.1 = (s32[64]{0:T(128)S(1)}, s32[64]{0:T(128)}, u32[]{:S(2)}) copy-start(s32[64]{0:T(128)} %param.19) | copy-start | bytes 772
  202.2 10.4 %copy-start.26 = (f32[16]{0:T(128)S(1)}, f32[16]{0:T(128)}, u32[]{:S(2)}) copy-start(f32[16]{0:T(128)} %param.29) | copy-start | bytes 196
  202.2 11.0 %copy-start.13 = (bf16[4,128]{1,0:T(4,128)(2,1)S(1)}, bf16[4,128]{1,0:T(4,128)(2,1)}, u32[]{:S(2)}) copy-start(bf16[4,128]{1,0:T(4,128)(2,1)} %param.26) | copy-start | bytes 3076
  202.2 11.6 %copy-start.14 = (bf16[4,128]{1,0:T(4,128)(2,1)S(1)}, bf16[4,128]{1,0:T(4,128)(2,1)}, u32[]{:S(2)}) copy-start(bf16[4,128]{1,0:T(4,128)(2,1)} %param.25) | copy-start | bytes 3076
  202.2 12.8 %copy-start.7 = (bf16[4,1024]{1,0:T(4,128)(2,1)S(1)}, bf16[4,1024]{1,0:T(4,128)(2,1)}, u32[]{:S(2)}) copy-start(bf16[4,1024]{1,0:T(4,128)(2,1)} %param.24) | copy-start | bytes 24580
  202.2 278.1 %all-to-all-start = ((bf16[64,32,4096]{2,1,0:T(8,128)(2,1)}), bf16[64,32,4096]{2,1,0:T(8,128)(2,1)}, u32[]{:S(2)}, u32[]{:S(2)}) async-start(bf16[64,32,4096]{2,1,0:T(8,128)(2,1)} %select_select_fusion), calls=%async_computation | async-start | bytes 33554432 | tf_op jit(solution)/shard_map/all_to_all | solution.py:118
  510.4 24.3 %copy-start.8 = (f32[1,1024]{1,0:T(1,128)S(1)}, f32[1,1024]{1,0:T(1,128)}, u32[]{:S(2)}) copy-start(f32[1,1024]{1,0:T(1,128)} %get-tuple-element.5) | copy-start | bytes 12292
  510.5 24.3 %copy-start.9 = (f32[1,1024]{1,0:T(1,128)S(1)}, f32[1,1024]{1,0:T(1,128)}, u32[]{:S(2)}) copy-start(f32[1,1024]{1,0:T(1,128)} %get-tuple-element.6) | copy-start | bytes 12292
  510.5 24.3 %copy-start.10 = (f32[1,1024]{1,0:T(1,128)S(1)}, f32[1,1024]{1,0:T(1,128)}, u32[]{:S(2)}) copy-start(f32[1,1024]{1,0:T(1,128)} %get-tuple-element.7) | copy-start | bytes 12292
  510.5 24.3 %copy-start.11 = (f32[1,1024]{1,0:T(1,128)S(1)}, f32[1,1024]{1,0:T(1,128)}, u32[]{:S(2)}) copy-start(f32[1,1024]{1,0:T(1,128)} %get-tuple-element.8) | copy-start | bytes 12292
  564.4 13.4 %copy-start.6 = (bf16[4096,16]{0,1:T(8,128)(2,1)S(1)}, bf16[4096,16]{0,1:T(8,128)(2,1)}, u32[]{:S(2)}) copy-start(bf16[4096,16]{0,1:T(8,128)(2,1)} %param.23) | copy-start | bytes 393220
  564.4 13.4 %copy-start.15 = (f32[16]{0:T(128)S(1)}, f32[16]{0:T(128)}, u32[]{:S(2)}) copy-start(f32[16]{0:T(128)} %param.30) | copy-start | bytes 196
  577.8 14.9 %copy-start.24 = (f32[16]{0:T(128)S(1)}, f32[16]{0:T(128)}, u32[]{:S(2)}) copy-start(f32[16]{0:T(128)} %exponential_negate_fusion) | copy-start | bytes 196
  597.6 8.3 %copy-start.20 = (f32[128]{0:T(128)S(1)}, f32[128]{0:T(128)}, u32[]{:S(2)}) copy-start(f32[128]{0:T(128)} %get-tuple-element.13) | copy-start | bytes 1540
  597.7 8.3 %copy-start.21 = (f32[128]{0:T(128)S(1)}, f32[128]{0:T(128)}, u32[]{:S(2)}) copy-start(f32[128]{0:T(128)} %get-tuple-element.14) | copy-start | bytes 1540
  597.7 8.3 %copy-start.22 = (f32[128]{0:T(128)S(1)}, f32[128]{0:T(128)}, u32[]{:S(2)}) copy-start(f32[128]{0:T(128)} %get-tuple-element.15) | copy-start | bytes 1540
  597.7 8.3 %copy-start.23 = (f32[128]{0:T(128)S(1)}, f32[128]{0:T(128)}, u32[]{:S(2)}) copy-start(f32[128]{0:T(128)} %get-tuple-element.16) | copy-start | bytes 1540
  597.7 9.0 %copy-start.25 = (bf16[4096,128]{1,0:T(8,128)(2,1)S(1)}, bf16[4096,128]{1,0:T(8,128)(2,1)}, u32[]{:S(2)}) copy-start(bf16[4096,128]{1,0:T(8,128)(2,1)} %param.21) | copy-start | bytes 3145732
  606.0 12.3 %slice-start = ((s8[8388608]{0:T(1024)(128)(4,1)}), s8[4194304]{0:T(1024)(128)(4,1)S(1)}, s32[]{:S(2)}) async-start(s8[8388608]{0:T(1024)(128)(4,1)} %bitcast.80), calls=%async_computation.3 | async-start | bytes 8388608
  606.6 8.6 %copy-start.16 = (f32[128]{0:T(128)S(1)}, f32[128]{0:T(128)}, u32[]{:S(2)}) copy-start(f32[128]{0:T(128)} %get-tuple-element.9) | copy-start | bytes 1540
  606.7 8.6 %copy-start.17 = (f32[128]{0:T(128)S(1)}, f32[128]{0:T(128)}, u32[]{:S(2)}) copy-start(f32[128]{0:T(128)} %get-tuple-element.10) | copy-start | bytes 1540
  606.7 8.6 %copy-start.18 = (f32[128]{0:T(128)S(1)}, f32[128]{0:T(128)}, u32[]{:S(2)}) copy-start(f32[128]{0:T(128)} %get-tuple-element.11) | copy-start | bytes 1540
  606.7 8.6 %copy-start.19 = (f32[128]{0:T(128)S(1)}, f32[128]{0:T(128)}, u32[]{:S(2)}) copy-start(f32[128]{0:T(128)} %get-tuple-element.12) | copy-start | bytes 1540
  606.7 11.6 %slice-start.1 = ((s8[8388608]{0:T(1024)(128)(4,1)}), s8[4194304]{0:T(1024)(128)(4,1)S(1)}, s32[]{:S(2)}) async-start(s8[8388608]{0:T(1024)(128)(4,1)} %bitcast.80), calls=%async_computation.4 | async-start | bytes 8388608
  606.7 11.6 %copy-start.12 = (pred[128,128]{1,0:T(8,128)(4,1)S(1)}, pred[128,128]{1,0:T(8,128)(4,1)}, u32[]{:S(2)}) copy-start(pred[128,128]{1,0:T(8,128)(4,1)} %fusion.55) | copy-start | bytes 49156
  606.7 11.6 %copy-start.27 = (f32[16]{0:T(128)S(1)}, f32[16]{0:T(128)}, u32[]{:S(2)}) copy-start(f32[16]{0:T(128)} %param.31) | copy-start | bytes 196
Sparse Core Ops, SparseCore 0:
  9.6 53.4 all-gather.2
  104.7 54.4 all-gather.4
